TPU v7x, 32 devices: a whole 2x2x4 slice. The times are simulated.
32 devices in a mesh: expert: 16 (over z, y, x), dp: 2 (over core).
Axes of the slice: x: 2, y: 2, z: 4, core: 2. Of those that a mesh axis runs over, the one named last changes fastest.
Arguments:
- tokens: bfloat16 [256, 3584], P('expert', 'dp'), may hold values from -6 to 6
- expert_ids: int32 [256, 8], P('expert'), may hold values from 0 to 15, all different within a row; in each aligned block of 16 rows (0 to 15, 16 to 31, ...) at most 16 rows name the same one
- route_weight: float32 [256, 8], P('expert'), may hold values from 0.1 to 1
- swap_flags: int32 [8], replicated, may hold values from 0 to 1, as said below
- w_gate: bfloat16 [16, 1024, 3584], P('expert', None, 'dp'), may hold values from -0.09375 to 0.09375
- w_up: bfloat16 [16, 1024, 3584], P('expert', None, 'dp'), may hold values from -0.09375 to 0.09375
- w_down: bfloat16 [16, 1024, 3584], P('expert', None, 'dp'), may hold values from -0.1875 to 0.1875
- cotangent: bfloat16 [256, 3584], P('expert', 'dp'), may hold values from -0.75 to 0.75
Outputs:
- mixed: bfloat16 [256, 3584], P('expert', 'dp')
- input_grad: bfloat16 [256, 3584], P('expert', 'dp')
- grad_gate: bfloat16 [16, 1024, 3584], P('expert', None, 'dp')
- grad_up: bfloat16 [16, 1024, 3584], P('expert', None, 'dp')
- grad_down: bfloat16 [16, 1024, 3584], P('expert', None, 'dp')
Inputs may be any that keep to these rules, and one draw needn't show every extreme that they name: `expert_ids`: in the 16 rows of one index of the expert axis (aligned blocks), each expert is named by at most 16 rows, a bound that some block reaches; a row names 8 different experts. `swap_flags`: entry p is 1 where slots p and p + 8 hold each other's experts; entry 0 is always 1, the others are 0 or 1.
All inputs are finite; a program needn't handle non-finite values.
Results may differ from a plain program's by a relative error of at most 0.0065.
Values may be sent and summed in bfloat16 or wider, within the bound.
A program may use at most 64 MiB of HBM per device.

v0:
```python
import jax
import jax.numpy as jnp
from jax import lax
from jax.sharding import PartitionSpec as P


def swapped(value, axis, apart):
    mask = 2**apart
    pairs = [(source, source ^ mask) for source in range(lax.axis_size(axis))]
    return lax.ppermute(value, axis, pairs)


def silu_parts(pre_gate):
    sigma = jax.nn.sigmoid(pre_gate)
    return (pre_gate * sigma, sigma * (1.0 + pre_gate * (1.0 - sigma)))


def contract_first(left_side, right_side):
    return lax.dot_general(
        left_side, right_side, (((0,), (0,)), ((), ())), preferred_element_type=jnp.float32
    )


def contract_last(left_side, right_side):
    return lax.dot_general(
        left_side, right_side, (((1,), (1,)), ((), ())), preferred_element_type=jnp.float32
    )


def per_device(tokens, expert_ids, route_weight, swap_flags, w_gate, w_up, w_down, cotangent):
    experts = lax.axis_size("expert")
    half_axis = experts // 2
    top_bit = half_axis.bit_length() - 1
    my_index = lax.axis_index("expert")
    shards = lax.axis_size("dp")
    dp_index = lax.axis_index("dp")
    tok_count, feat_width = tokens.shape
    top_count = expert_ids.shape[1]
    capacity = min(tok_count, max(2, 2 * tok_count * top_count // experts))
    row_total = tok_count * top_count
    slot_total = experts * capacity
    hidden_width = w_gate.shape[1]
    share_width = hidden_width // shards
    flat_ids = expert_ids.reshape(row_total)
    expert_cols = jnp.arange(experts, dtype=jnp.int32)
    id_match = (flat_ids[:, None] == expert_cols[None, :]).astype(jnp.int32)
    row_rank = jnp.sum(jnp.cumsum(id_match, axis=0) * id_match, axis=1) - 1
    own_weights = (w_gate[0], w_up[0], w_down[0])
    my_flag = swap_flags[my_index % half_axis]
    flipped = swap_flags[flat_ids % half_axis] == 1
    target = jnp.where(flipped, (flat_ids + half_axis) % experts, flat_ids)
    partner_weights = swapped((own_weights[0], own_weights[1], own_weights[2]), "expert", top_bit)
    gate_w, up_w, down_w = tuple(
        (
            jnp.where(my_flag == 1, their_part, own_part)
            for their_part, own_part in zip(partner_weights, own_weights)
        )
    )
    slot_index = target * capacity + row_rank
    placing = (jnp.arange(slot_total, dtype=jnp.int32)[:, None] == slot_index[None, :]).astype(
        jnp.bfloat16
    )

    def trade(outbound):
        moved = lax.all_to_all(
            outbound.reshape(experts, capacity, feat_width),
            "expert",
            split_axis=0,
            concat_axis=0,
            tiled=True,
        )
        return moved.reshape(slot_total, feat_width)

    def dispatch(row_data):
        return trade(
            jnp.dot(placing, row_data, preferred_element_type=jnp.float32).astype(jnp.bfloat16)
        )

    def collect(slot_data):
        returned = trade(slot_data)
        return contract_first(placing, returned).reshape(tok_count, top_count, feat_width)

    token_rows = jnp.broadcast_to(tokens[:, None, :], (tok_count, top_count, feat_width)).reshape(
        row_total, feat_width
    )
    in_rows = dispatch(token_rows)
    gate_part = contract_last(in_rows, gate_w)
    up_part = contract_last(in_rows, up_w)
    pre_gate, up_value = lax.psum((gate_part, up_part), "dp")
    activated, slope = silu_parts(pre_gate)
    hidden = (activated * up_value).astype(jnp.bfloat16)
    first_unit = dp_index * share_width
    act_share = lax.dynamic_slice_in_dim(activated, first_unit, share_width, 1)
    slope_share = lax.dynamic_slice_in_dim(slope, first_unit, share_width, 1)
    up_share = lax.dynamic_slice_in_dim(up_value, first_unit, share_width, 1)
    expert_out = jnp.dot(hidden, down_w, preferred_element_type=jnp.float32).astype(jnp.bfloat16)
    out_rows = collect(expert_out)
    mixed = jnp.sum(route_weight[:, :, None] * out_rows, axis=1).astype(jnp.bfloat16)
    scaled = route_weight[:, :, None] * cotangent.astype(jnp.float32)[:, None, :]
    grad_in = dispatch(scaled.reshape(row_total, feat_width).astype(jnp.bfloat16))
    hidden_grad = lax.psum_scatter(
        contract_last(grad_in, down_w), "dp", scatter_dimension=1, tiled=True
    )
    gate_grad_share = (hidden_grad * up_share * slope_share).astype(jnp.bfloat16)
    up_grad_share = (hidden_grad * act_share).astype(jnp.bfloat16)
    gate_grad, up_grad = (
        lax.all_gather(gate_grad_share, "dp", axis=1, tiled=True),
        lax.all_gather(up_grad_share, "dp", axis=1, tiled=True),
    )
    grads = (
        contract_first(gate_grad, in_rows).astype(jnp.bfloat16),
        contract_first(up_grad, in_rows).astype(jnp.bfloat16),
        contract_first(hidden, grad_in).astype(jnp.bfloat16),
    )
    row_back = (
        jnp.dot(gate_grad, gate_w, preferred_element_type=jnp.float32)
        + jnp.dot(up_grad, up_w, preferred_element_type=jnp.float32)
    ).astype(jnp.bfloat16)
    back_rows = collect(row_back)
    input_grad = jnp.sum(back_rows, axis=1).astype(jnp.bfloat16)
    return (mixed, input_grad, grads[0][None], grads[1][None], grads[2][None])


def solution(mesh):
    return jax.shard_map(
        per_device,
        mesh=mesh,
        in_specs=(
            P("expert", "dp"),
            P("expert", None),
            P("expert", None),
            P(),
            P("expert", None, "dp"),
            P("expert", None, "dp"),
            P("expert", None, "dp"),
            P("expert", "dp"),
        ),
        out_specs=(
            P("expert", "dp"),
            P("expert", "dp"),
            P("expert", None, "dp"),
            P("expert", None, "dp"),
            P("expert", None, "dp"),
        ),
        check_vma=False,
    )
```

profile of v0, /device:TPU:0, one launch (start us, length us, event | category | flops | bytes accessed | tf_op | source)
XLA Modules:
  0.0 599.8 jit_solution(2162964550452987924)
XLA Ops:
  7.2 0.0 copy-start
  7.2 4.1 collective-permute-start.1
  11.3 0.1 collective-permute-start
  11.4 0.8 copy.18
  12.1 0.1 reshape.181
  12.2 0.1 reshape.180
  12.3 0.1 fusion.26
  12.4 0.2 reduce_window_sum.11
  12.6 1.6 fusion.37
  14.2 0.2 select_reduce_fusion
  14.4 5.1 add_add_fusion
  19.5 0.0 copy-done
  19.5 1.3 convolution_convert_fusion.4
  20.8 7.1 %all-to-all-start = ((bf16[16,16,1792]{2,1,0:T(8,128)(2,1)}), bf16[16,16,1792]{2,1,0:T(8,128)(2,1)S(1)}, u32[]{:S(2)}, u32[]{:S(2)}) async-start(bf16[16,16,1792]{2,1,0:T(8,128)(2,1)} %bitcast.12), calls=%async_computation | async-start | bytes 1835008 | tf_op jit(solution)/shard_map/all_to_all | solution.py:65
  28.0 2.8 collective-permute-start.2
  30.8 0.8 copy.17
  31.6 0.8 convert_element_type.51
  32.4 0.1 mul.67
  33.1 1.4 convolution_convert_fusion.3
  34.5 389.9 %all-to-all-done = bf16[16,16,1792]{2,1,0:T(8,128)(2,1)S(1)} async-done(((bf16[16,16,1792]{2,1,0:T(8,128)(2,1)}), bf16[16,16,1792]{2,1,0:T(8,128)(2,1)S(1)}, u32[]{:S(2)}, u32[]{:S(2)}) %all-to-all-start) | async-done | bytes 917536 | tf_op jit(solution)/shard_map/all_to_all | solution.py:65
  424.5 7.5 %all-to-all-start.2 = ((bf16[16,16,1792]{2,1,0:T(8,128)(2,1)}), bf16[16,16,1792]{2,1,0:T(8,128)(2,1)S(1)}, u32[]{:S(2)}, u32[]{:S(2)}) async-start(bf16[16,16,1792]{2,1,0:T(8,128)(2,1)} %bitcast.22), calls=%async_computation.2 | async-start | bytes 1835008 | tf_op jit(solution)/shard_map/all_to_all | solution.py:65
  431.9 0.0 all-reduce.3.cloned.1.call-start
  432.0 0.0 collective-permute-done.1
  432.0 0.0 copy-start.11
  432.0 5.5 fusion.6
  437.5 0.0 collective-permute-done
  437.5 0.0 copy-done.3
  437.5 0.0 copy-done.11
  437.5 4.2 fusion.4
  441.7 0.0 all-reduce.3.cloned.1.call-update
  441.7 0.0 reduce-scatter.2.cloned.1.call-start
  441.8 81.0 %all-to-all-done.2 = bf16[16,16,1792]{2,1,0:T(8,128)(2,1)S(1)} async-done(((bf16[16,16,1792]{2,1,0:T(8,128)(2,1)}), bf16[16,16,1792]{2,1,0:T(8,128)(2,1)S(1)}, u32[]{:S(2)}, u32[]{:S(2)}) %all-to-all-start.2) | async-done | bytes 917536 | tf_op jit(solution)/shard_map/all_to_all | solution.py:65
  522.8 0.0 collective-permute-done.2
  522.8 5.7 fusion.7
  528.5 0.0 copy-done.5
  528.5 0.0 reduce-scatter.2.cloned.1.call-update
  528.5 0.0 all-reduce.3.cloned.1.call-done
  528.5 0.0 copy-start.9
  528.5 3.1 add_divide_fusion
  531.6 0.0 copy-done.9
  531.6 4.4 convolution_convert_fusion.5
  536.0 0.0 copy-done.7
  536.0 7.4 %all-to-all-start.1 = ((bf16[16,16,1792]{2,1,0:T(8,128)(2,1)}), bf16[16,16,1792]{2,1,0:T(8,128)(2,1)}, u32[]{:S(2)}, u32[]{:S(2)}) async-start(bf16[16,16,1792]{2,1,0:T(8,128)(2,1)} %bitcast.101), calls=%async_computation.1 | async-start | bytes 1835008 | tf_op jit(solution)/shard_map/all_to_all | solution.py:65
  543.4 0.0 reduce-scatter.2.cloned.1.call-done
  543.4 0.0 copy-start.10
  543.5 0.0 copy-done.1
  543.5 0.0 copy-done.2
  543.5 1.7 fusion.13
  545.2 2.2 all_gather.7
  547.4 2.2 all_gather.6
  549.5 0.0 copy-done.10
  549.5 3.4 fusion.5
  553.0 0.0 copy-done.12
  553.0 0.0 copy-start.4
  553.0 4.4 fusion.3
  557.3 8.3 %all-to-all-done.1 = bf16[16,16,1792]{2,1,0:T(8,128)(2,1)} async-done(((bf16[16,16,1792]{2,1,0:T(8,128)(2,1)}), bf16[16,16,1792]{2,1,0:T(8,128)(2,1)}, u32[]{:S(2)}, u32[]{:S(2)}) %all-to-all-start.1) | async-done | bytes 917536 | tf_op jit(solution)/shard_map/all_to_all | solution.py:65
  565.7 5.5 all-to-all-start.3
  571.1 3.0 fusion
  574.1 3.0 fusion.1
  577.2 0.0 copy-done.8
  577.2 3.0 fusion.2
  580.2 2.3 fusion.8
  582.4 9.4 %all-to-all-done.3 = bf16[16,16,1792]{2,1,0:T(8,128)(2,1)S(1)} async-done(((bf16[16,16,1792]{2,1,0:T(8,128)(2,1)}), bf16[16,16,1792]{2,1,0:T(8,128)(2,1)S(1)}, u32[]{:S(2)}, u32[]{:S(2)}) %all-to-all-start.3) | async-done | bytes 917536 | tf_op jit(solution)/shard_map/all_to_all | solution.py:65
  591.9 1.1 convolution_reduce_fusion
  (10 shorter events, 0.0 us)
Async XLA Ops:
  7.2 12.3 %copy-start = (bf16[16,1792]{1,0:T(8,128)(2,1)S(1)}, bf16[16,1792]{1,0:T(8,128)(2,1)}, u32[]{:S(2)}) copy-start(bf16[16,1792]{1,0:T(8,128)(2,1)} %param.8) | copy-start | bytes 172036
  7.2 424.8 %collective-permute-start.1 = (bf16[1024,1792]{1,0:T(8,128)(2,1)}, bf16[1024,1792]{1,0:T(8,128)(2,1)}, u32[]{:S(2)}, u32[]{:S(2)}) collective-permute-start(bf16[1024,1792]{1,0:T(8,128)(2,1)} %bitcast.103), channel_id=1, source_target_pairs={{0,16},{2,18},{4,20},{6,22},{8,24},{10,26},{12,28},{14,30},{16,0},... | collective-permute-start | bytes 11010056 | tf_op jit(solution)/shard_map/ppermute | solution.py:10
  11.3 426.2 %collective-permute-start = (bf16[1024,1792]{1,0:T(8,128)(2,1)}, bf16[1024,1792]{1,0:T(8,128)(2,1)}, u32[]{:S(2)}, u32[]{:S(2)}) collective-permute-start(bf16[1024,1792]{1,0:T(8,128)(2,1)} %bitcast.104), channel_id=1, source_target_pairs={{0,16},{2,18},{4,20},{6,22},{8,24},{10,26},{12,28},{14,30},{16,0},... | collective-permute-start | bytes 11010056 | tf_op jit(solution)/shard_map/ppermute | solution.py:10
  20.8 403.6 %all-to-all-start = ((bf16[16,16,1792]{2,1,0:T(8,128)(2,1)}), bf16[16,16,1792]{2,1,0:T(8,128)(2,1)S(1)}, u32[]{:S(2)}, u32[]{:S(2)}) async-start(bf16[16,16,1792]{2,1,0:T(8,128)(2,1)} %bitcast.12), calls=%async_computation | async-start | bytes 1835008 | tf_op jit(solution)/shard_map/all_to_all | solution.py:65
  28.0 494.8 %collective-permute-start.2 = (bf16[1024,1792]{1,0:T(8,128)(2,1)}, bf16[1024,1792]{1,0:T(8,128)(2,1)}, u32[]{:S(2)}, u32[]{:S(2)}) collective-permute-start(bf16[1024,1792]{1,0:T(8,128)(2,1)} %bitcast.102), channel_id=1, source_target_pairs={{0,16},{2,18},{4,20},{6,22},{8,24},{10,26},{12,28},{14,30},{16,0},... | collective-permute-start | bytes 11010056 | tf_op jit(solution)/shard_map/ppermute | solution.py:10
  424.5 13.0 %copy-start.3 = (bf16[16,16,1792]{2,1,0:T(8,128)(2,1)}, bf16[16,16,1792]{2,1,0:T(8,128)(2,1)S(1)}, u32[]{:S(2)}) copy-start(bf16[16,16,1792]{2,1,0:T(8,128)(2,1)S(1)} %all-to-all-done) | copy-start | bytes 2752516
  424.5 98.3 %all-to-all-start.2 = ((bf16[16,16,1792]{2,1,0:T(8,128)(2,1)}), bf16[16,16,1792]{2,1,0:T(8,128)(2,1)S(1)}, u32[]{:S(2)}, u32[]{:S(2)}) async-start(bf16[16,16,1792]{2,1,0:T(8,128)(2,1)} %bitcast.22), calls=%async_computation.2 | async-start | bytes 1835008 | tf_op jit(solution)/shard_map/all_to_all | solution.py:65
  431.9 96.6 %all-reduce.3.cloned.1.call-start = ((), (), s32[]{:S(2)}) async-start(), calls=%async_computation.6 | async-start | bytes 4194304 | tf_op jit(solution)/shard_map/psum | solution.py:89
  432.0 5.5 copy-start.11
  441.7 101.7 %reduce-scatter.2.cloned.1.call-start = ((), (), s32[]{:S(2)}) async-start(), calls=%async_computation.5 | async-start | bytes 1572864 | tf_op jit(solution)/shard_map/reduce_scatter | solution.py:101
  522.8 5.7 copy-start.5
  528.5 3.1 copy-start.9
  531.6 4.4 copy-start.7
  531.6 11.9 %copy-start.1 = (f32[256,1024]{1,0:T(8,128)S(1)}, f32[256,1024]{1,0:T(8,128)}, u32[]{:S(2)}) copy-start(f32[256,1024]{1,0:T(8,128)} %get-tuple-element.5) | copy-start | bytes 3145732
  531.6 11.9 %copy-start.2 = (f32[256,1024]{1,0:T(8,128)S(1)}, f32[256,1024]{1,0:T(8,128)}, u32[]{:S(2)}) copy-start(f32[256,1024]{1,0:T(8,128)} %get-tuple-element.6) | copy-start | bytes 3145732
  536.0 29.6 %all-to-all-start.1 = ((bf16[16,16,1792]{2,1,0:T(8,128)(2,1)}), bf16[16,16,1792]{2,1,0:T(8,128)(2,1)}, u32[]{:S(2)}, u32[]{:S(2)}) async-start(bf16[16,16,1792]{2,1,0:T(8,128)(2,1)} %bitcast.101), calls=%async_computation.1 | async-start | bytes 1835008 | tf_op jit(solution)/shard_map/all_to_all | solution.py:65
  543.4 6.1 %copy-start.10 = (bf16[1,1024,1792]{2,1,0:T(8,128)(2,1)S(1)}, bf16[1,1024,1792]{2,1,0:T(8,128)(2,1)}, u32[]{:S(2)}) copy-start(bf16[1,1024,1792]{2,1,0:T(8,128)(2,1)} %param.13) | copy-start | bytes 11010052
  549.5 3.4 copy-start.12
  553.0 18.2 %copy-start.4 = (bf16[16,16,1792]{2,1,0:T(8,128)(2,1)S(1)}, bf16[16,16,1792]{2,1,0:T(8,128)(2,1)}, u32[]{:S(2)}) copy-start(bf16[16,16,1792]{2,1,0:T(8,128)(2,1)} %copy-done.3) | copy-start | bytes 2752516
  565.7 26.2 %all-to-all-start.3 = ((bf16[16,16,1792]{2,1,0:T(8,128)(2,1)}), bf16[16,16,1792]{2,1,0:T(8,128)(2,1)S(1)}, u32[]{:S(2)}, u32[]{:S(2)}) async-start(bf16[16,16,1792]{2,1,0:T(8,128)(2,1)} %bitcast.24), calls=%async_computation.4 | async-start | bytes 1835008 | tf_op jit(solution)/shard_map/all_to_all | solution.py:65
  574.1 3.0 copy-start.6
  574.1 3.0 copy-start.8
Sparse Core Ops, SparseCore 0:
  441.9 21.6 all-reduce.2
  528.6 10.2 reduce-scatter.1
where the time goes:
time: 601 us; the launch traced here: 600 us
  waiting for transfers between devices  489 us (81%)
  matrix products  42.6 us (7%)
  starting transfers between devices  34.5 us (6%)
  between operations  14.9 us (2%)
  other arithmetic  11.1 us (2%)
    all_to_all x4, waiting for transfers between devices, trade(): lax.all_to_all(outbound.reshape(experts, capacity, feat_width), 'expert',...  489 us
    all_to_all x4, starting transfers between devices, trade(): lax.all_to_all(outbound.reshape(experts, capacity, feat_width), 'expert',...  27.4 us
    dot_general x3, matrix products, contract_last(): lax.dot_general(left_side, right_side, (((1,), (1,)), ((), ())), preferre...  15.4 us
    dot_general x5, matrix products, contract_first(): lax.dot_general(left_side, right_side, (((0,), (0,)), ((), ())), preferre...  12.4 us
  transfers between devices with their start and end apart: 9, of which 4 were waited for; matrix products, arithmetic and copies ran while one was open for 9% of the time, Pallas kernels for 0%

commit v1 on v0

v1 whole, which is shorter than its diff:
```python
import jax
import jax.numpy as jnp
from jax import lax
from jax.sharding import PartitionSpec as P


def silu_parts(pre_gate):
    sigma = jax.nn.sigmoid(pre_gate)
    return (pre_gate * sigma, sigma * (1.0 + pre_gate * (1.0 - sigma)))


def contract_first(left_side, right_side):
    return lax.dot_general(
        left_side, right_side, (((0,), (0,)), ((), ())), preferred_element_type=jnp.float32
    )


def contract_last(left_side, right_side):
    return lax.dot_general(
        left_side, right_side, (((1,), (1,)), ((), ())), preferred_element_type=jnp.float32
    )


def per_device(tokens, expert_ids, route_weight, swap_flags, w_gate, w_up, w_down, cotangent):
    experts = lax.axis_size("expert")
    half_axis = experts // 2
    my_index = lax.axis_index("expert")
    my_flag = swap_flags[my_index % half_axis] == 1
    gate_w, up_w, down_w = w_gate[0], w_up[0], w_down[0]
    pairs = [(source, (source + half_axis) % experts) for source in range(experts)]

    chosen = lax.all_gather(expert_ids, "expert", axis=0, tiled=True) == my_index
    weights = lax.all_gather(route_weight, "expert", axis=0, tiled=True)
    in_rows = lax.all_gather(tokens, "expert", axis=0, tiled=True)
    grad_rows = lax.all_gather(cotangent, "expert", axis=0, tiled=True)
    weight = jnp.sum(jnp.where(chosen, weights, 0.0), axis=1, keepdims=True)
    picked = jnp.any(chosen, axis=1, keepdims=True)

    def share_sum(part):
        return lax.psum_scatter(part, "dp", scatter_dimension=1, tiled=True)

    def whole(share):
        return lax.all_gather(share, "dp", axis=1, tiled=True)

    pre_gate = share_sum(contract_last(in_rows, gate_w))
    up_value = share_sum(contract_last(in_rows, up_w))
    activated, slope = silu_parts(pre_gate)
    hidden = jnp.where(picked, activated * up_value, 0.0)
    weighted = (weight * hidden).astype(jnp.bfloat16)
    hidden = hidden.astype(jnp.bfloat16)
    out_part = weight * jnp.dot(whole(hidden), down_w, preferred_element_type=jnp.float32)
    mixed = lax.psum_scatter(
        out_part.astype(jnp.bfloat16), "expert", scatter_dimension=0, tiled=True
    )
    hidden_grad = weight * share_sum(contract_last(grad_rows, down_w))
    gate_grad = (hidden_grad * up_value * slope).astype(jnp.bfloat16)
    up_grad = (hidden_grad * activated).astype(jnp.bfloat16)
    back_part = jnp.dot(
        whole(gate_grad), gate_w, preferred_element_type=jnp.float32
    ) + jnp.dot(whole(up_grad), up_w, preferred_element_type=jnp.float32)
    input_grad = lax.psum_scatter(
        back_part.astype(jnp.bfloat16), "expert", scatter_dimension=0, tiled=True
    )

    def held(share):
        return whole(jnp.where(my_flag, lax.ppermute(share, "expert", pairs), share))

    grads = (
        contract_first(held(gate_grad), in_rows).astype(jnp.bfloat16),
        contract_first(held(up_grad), in_rows).astype(jnp.bfloat16),
        contract_first(held(weighted), grad_rows).astype(jnp.bfloat16),
    )
    return (mixed, input_grad, grads[0][None], grads[1][None], grads[2][None])


def solution(mesh):
    return jax.shard_map(
        per_device,
        mesh=mesh,
        in_specs=(
            P("expert", "dp"),
            P("expert", None),
            P("expert", None),
            P(),
            P("expert", None, "dp"),
            P("expert", None, "dp"),
            P("expert", None, "dp"),
            P("expert", "dp"),
        ),
        out_specs=(
            P("expert", "dp"),
            P("expert", "dp"),
            P("expert", None, "dp"),
            P("expert", None, "dp"),
            P("expert", None, "dp"),
        ),
        check_vma=False,
    )
```

time: 601 us -> 351 us (0.58)
  waiting for transfers between devices: 489 us -> 123 us
  blocking collectives: 4.35 us -> 176 us
  starting transfers between devices: 34.5 us -> 3.27 us
  matrix products: 42.6 us -> 30.9 us
  other arithmetic: 11.1 us -> 1.85 us
    all_to_all x4 -> x0, waiting for transfers between devices: 489 us -> none  [trade(): lax.all_to_all(outbound.reshape(experts, capacity, feat_width), 'expert',...]
    all_gather x2 -> x10, blocking collectives: 4.35 us -> 176 us  [the longest x1 48.1 us: per_device(): grad_rows = lax.all_gather(cotangent, 'expert', axis=0, tiled=True)]
    reduce_scatter x1 -> x5, waiting for transfers between devices: 0.02 us -> 104 us  [the longest x1 76.9 us: per_device(): lax.psum_scatter(back_part.astype(jnp.bfloat16), 'expert', scatter_dimens...]
    all_to_all x4 -> x0, starting transfers between devices: 27.4 us -> none  [trade(): lax.all_to_all(outbound.reshape(experts, capacity, feat_width), 'expert',...]
    ppermute x3, waiting for transfers between devices: 0.01 us -> 19 us  [held(): lax.ppermute(share, 'expert', pairs)]
    dot_general x5 -> x3, matrix products: 14.9 us -> 9.35 us  [the longest x1 4.1 us: per_device(): jnp.dot(whole(hidden), down_w, preferred_element_type=jnp.float32)]
    dot_general x5 -> x3, matrix products: 12.4 us -> 9.04 us  [contract_first(): lax.dot_general(left_side, right_side, (((0,), (0,)), ((), ())), preferre...]
  transfers between devices with their start and end apart: 9 -> 8, of which waited for: 4 -> 5; matrix products, arithmetic and copies ran while one was open for 9% -> 7% of each run, Pallas kernels for 0% -> 0%
where the time goes in v1:
time: 351 us
  blocking collectives  176 us (50%)
  waiting for transfers between devices  123 us (35%)
  matrix products  30.9 us (9%)
  between operations  14.6 us (4%)
    reduce_scatter x1, waiting for transfers between devices, per_device(): lax.psum_scatter(back_part.astype(jnp.bfloat16), 'expert', scatter_dimens...  76.9 us
    all_gather x1, blocking collectives, per_device(): grad_rows = lax.all_gather(cotangent, 'expert', axis=0, tiled=True)  48.1 us
    all_gather x1, blocking collectives, per_device(): in_rows = lax.all_gather(tokens, 'expert', axis=0, tiled=True)  40.9 us
    all_gather x1, blocking collectives, per_device(): lax.all_gather(expert_ids, 'expert', axis=0, tiled=True) == my_index  38.1 us
    all_gather x1, blocking collectives, per_device(): weights = lax.all_gather(route_weight, 'expert', axis=0, tiled=True)  35.8 us
    reduce_scatter x1, waiting for transfers between devices, per_device(): lax.psum_scatter(out_part.astype(jnp.bfloat16), 'expert', scatter_dimensi...  27.2 us
    ppermute x3, waiting for transfers between devices, held(): lax.ppermute(share, 'expert', pairs)  19 us
    all_gather x6, blocking collectives, whole(): return lax.all_gather(share, 'dp', axis=1, tiled=True)  13.2 us
  transfers between devices with their start and end apart: 8, of which 5 were waited for; matrix products, arithmetic and copies ran while one was open for 7% of the time, Pallas kernels for 0%

profile of v1, /device:TPU:0, one launch (start us, length us, event | category | flops | bytes accessed | tf_op | source)
XLA Modules:
  0.0 350.7 jit_solution(17655747263729802290)
XLA Ops:
  7.2 0.0 reduce-scatter.12.cloned.1.call-start
  7.2 48.1 %all_gather.34 = bf16[256,1792]{1,0:T(8,128)(2,1)S(1)} all-gather(bf16[16,1792]{1,0:T(8,128)(2,1)} %param.15), channel_id=1, replica_groups=mesh['expert'=16,'dp'=2] {'expert'}, dimensions={0}, use_global_device_ids=true | all-gather | bytes 974848 | tf_op jit(solution)/shard_map/all_gather | solution.py:35
  55.4 0.0 copy-start
  55.4 4.2 %fusion = f32[256,1024]{1,0:T(8,128)} fusion(bf16[256,1792]{1,0:T(8,128)(2,1)S(1)} %all_gather.34, bf16[1,1024,1792]{2,1,0:T(8,128)(2,1)} %param.14), kind=kOutput, calls=%fused_computation.3 | convolution fusion | flops 939524096 | bytes 5636096 | tf_op jit(solution)/shard_map/dot_general | solution.py:19
  59.5 0.0 reduce-scatter.12.cloned.1.call-update
  59.5 0.0 reduce-scatter.8.cloned.1.call-start
  59.6 0.0 copy-done
  59.6 40.9 %all_gather.32 = bf16[256,1792]{1,0:T(8,128)(2,1)S(1)} all-gather(bf16[16,1792]{1,0:T(8,128)(2,1)S(1)} %copy-done), channel_id=1, replica_groups=mesh['expert'=16,'dp'=2] {'expert'}, dimensions={0}, use_global_device_ids=true | all-gather | bytes 974848 | tf_op jit(solution)/shard_map/all_gather | solution.py:34
  100.5 4.2 %fusion.6 = f32[256,1024]{1,0:T(8,128)} fusion(bf16[256,1792]{1,0:T(8,128)(2,1)S(1)} %all_gather.32, bf16[1,1024,1792]{2,1,0:T(8,128)(2,1)} %param.13), kind=kOutput, calls=%fused_computation.9 | convolution fusion | flops 939524096 | bytes 5636096 | tf_op jit(solution)/shard_map/dot_general | solution.py:19
  104.6 0.0 reduce-scatter.8.cloned.1.call-update
  104.7 0.0 copy-start.1
  104.7 0.0 copy-start.2
  104.7 0.0 reduce-scatter.6.cloned.1.call-start
  104.7 4.2 %fusion.10 = f32[256,1024]{1,0:T(8,128)} fusion(bf16[256,1792]{1,0:T(8,128)(2,1)S(1)} %all_gather.32, bf16[1,1024,1792]{2,1,0:T(8,128)(2,1)} %param.12), kind=kOutput, calls=%fused_computation.13 | convolution fusion | flops 939524096 | bytes 5636096 | tf_op jit(solution)/shard_map/dot_general | solution.py:19
  108.9 0.0 reduce-scatter.6.cloned.1.call-update
  108.9 0.0 reduce-scatter.10.cloned.1.call-start
  109.0 0.0 copy-done.1
  109.0 38.1 %all-gather = s32[16,16,8]{1,2,0:T(8,128)S(1)} all-gather(s32[1,16,8]{1,2,0:T(8,128)S(1)} %bitcast.44), channel_id=1, replica_groups=mesh['expert'=16,'dp'=2] {'expert'}, dimensions={0}, use_global_device_ids=true | all-gather | bytes 8704 | tf_op jit(solution)/shard_map/all_gather | solution.py:32
  147.1 0.0 copy-done.2
  147.1 35.8 %all-gather.1 = f32[16,16,8]{1,2,0:T(8,128)S(1)} all-gather(f32[1,16,8]{1,2,0:T(8,128)S(1)} %bitcast.45), channel_id=1, replica_groups=mesh['expert'=16,'dp'=2] {'expert'}, dimensions={0}, use_global_device_ids=true | all-gather | bytes 8704 | tf_op jit(solution)/shard_map/all_gather | solution.py:33
  182.9 0.1 reshape.23
  183.1 0.1 reshape.20
  183.1 0.0 reduce-scatter.12.cloned.1.call-done
  183.2 0.0 reduce-scatter.8.cloned.1.call-done
  183.2 0.0 reduce-scatter.6.cloned.1.call-done
  183.2 1.7 multiply_convert_fusion.2
  184.9 2.2 all_gather.33
  187.1 0.0 copy-start.4
  187.1 4.1 %fusion.21 = bf16[256,1792]{1,0:T(8,128)(2,1)} fusion(bf16[256,1024]{1,0:T(8,128)(2,1)S(1)} %all_gather.33, bf16[1,1024,1792]{2,1,0:T(8,128)(2,1)} %param.14, f32[256]{0:T(256)S(1)} %reshape.23), kind=kOutput, calls=%fused_computation.20 | convolution fusion | flops 940441600 | bytes 5112832 | tf_op jit(solution)/shard_map/dot_general | solution.py:51
  191.2 0.0 reduce-scatter.10.cloned.1.call-update
  191.2 0.0 reduce-scatter.14.cloned.1.call-start
  191.3 0.0 copy-done.4
  191.3 0.6 dynamic_slice.3
  192.5 0.1 collective-permute-start.2
  192.6 2.9 collective-permute-start
  195.5 0.0 copy-start.3
  195.5 0.1 collective-permute-start.1
  195.6 2.3 all_gather.35
  197.9 2.2 all_gather.36
  200.1 3.1 fusion.4
  203.2 0.0 copy-done.3
  203.2 2.1 fusion.24
  205.3 0.0 reduce-scatter.14.cloned.1.call-update
  205.4 9.8 %collective-permute-done.2 = bf16[256,512]{1,0:T(8,128)(2,1)S(1)} collective-permute-done((bf16[256,512]{1,0:T(8,128)(2,1)S(1)}, bf16[256,512]{1,0:T(8,128)(2,1)S(1)}, u32[]{:S(2)}, u32[]{:S(2)}) %collective-permute-start.2) | collective-permute-done | bytes 262176 | tf_op jit(solution)/shard_map/ppermute | solution.py:66
  215.2 6.7 %collective-permute-done = bf16[256,512]{1,0:T(8,128)(2,1)S(1)} collective-permute-done((bf16[256,512]{1,0:T(8,128)(2,1)S(1)}, bf16[256,512]{1,0:T(8,128)(2,1)S(1)}, u32[]{:S(2)}, u32[]{:S(2)}) %collective-permute-start) | collective-permute-done | bytes 262176 | tf_op jit(solution)/shard_map/ppermute | solution.py:66
  222.0 2.2 all_gather.39
  224.1 2.2 all_gather.37
  226.3 2.5 collective-permute-done.1
  228.8 2.2 all_gather.38
  231.0 3.0 fusion.14
  234.0 3.0 fusion.13
  237.0 3.0 fusion.12
  240.0 27.2 %reduce-scatter.10.cloned.1.call-done = bf16[16,1792]{1,0:T(8,128)(2,1)} async-done(((bf16[256,1792]{1,0:T(8,128)(2,1)}), bf16[16,1792]{1,0:T(8,128)(2,1)}) %reduce-scatter.10.cloned.1.call-update) | async-done | bytes 57360 | tf_op jit(solution)/shard_map/reduce_scatter | solution.py:52
  267.2 76.9 %reduce-scatter.14.cloned.1.call-done = bf16[16,1792]{1,0:T(8,128)(2,1)} async-done(((bf16[256,1792]{1,0:T(8,128)(2,1)}), bf16[16,1792]{1,0:T(8,128)(2,1)}) %reduce-scatter.14.cloned.1.call-update) | async-done | bytes 57360 | tf_op jit(solution)/shard_map/reduce_scatter | solution.py:61
  (5 shorter events, 0.2 us)
Async XLA Ops:
  7.2 176.0 %reduce-scatter.12.cloned.1.call-start = ((), (), s32[]{:S(2)}) async-start(), calls=%async_computation.8 | async-start | bytes 1572864 | tf_op jit(solution)/shard_map/reduce_scatter | solution.py:40
  55.4 4.2 %copy-start = (bf16[16,1792]{1,0:T(8,128)(2,1)S(1)}, bf16[16,1792]{1,0:T(8,128)(2,1)}, u32[]{:S(2)}) copy-start(bf16[16,1792]{1,0:T(8,128)(2,1)} %param.8) | copy-start | bytes 172036
  59.5 123.6 %reduce-scatter.8.cloned.1.call-start = ((), (), s32[]{:S(2)}) async-start(), calls=%async_computation.6 | async-start | bytes 1572864 | tf_op jit(solution)/shard_map/reduce_scatter | solution.py:40
  104.7 4.3 %copy-start.1 = (s32[16,8]{0,1:T(8,128)S(1)}, s32[16,8]{0,1:T(8,128)}, u32[]{:S(2)}) copy-start(s32[16,8]{0,1:T(8,128)} %param.9) | copy-start | bytes 1540
  104.7 42.4 %copy-start.2 = (f32[16,8]{0,1:T(8,128)S(1)}, f32[16,8]{0,1:T(8,128)}, u32[]{:S(2)}) copy-start(f32[16,8]{0,1:T(8,128)} %param.10) | copy-start | bytes 1540
  104.7 78.5 %reduce-scatter.6.cloned.1.call-start = ((), (), s32[]{:S(2)}) async-start(), calls=%async_computation.5 | async-start | bytes 1572864 | tf_op jit(solution)/shard_map/reduce_scatter | solution.py:40
  108.9 158.3 %reduce-scatter.10.cloned.1.call-start = ((), (), s32[]{:S(2)}) async-start(), calls=%async_computation.7 | async-start | bytes 974848 | tf_op jit(solution)/shard_map/reduce_scatter | solution.py:52
  187.1 4.2 %copy-start.4 = (s32[8]{0:T(128)S(1)}, s32[8]{0:T(128)}, u32[]{:S(2)}) copy-start(s32[8]{0:T(128)} %param.11) | copy-start | bytes 100
  191.2 153.0 %reduce-scatter.14.cloned.1.call-start = ((), (), s32[]{:S(2)}) async-start(), calls=%async_computation.9 | async-start | bytes 974848 | tf_op jit(solution)/shard_map/reduce_scatter | solution.py:61
  192.5 22.6 %collective-permute-start.2 = (bf16[256,512]{1,0:T(8,128)(2,1)S(1)}, bf16[256,512]{1,0:T(8,128)(2,1)S(1)}, u32[]{:S(2)}, u32[]{:S(2)}) collective-permute-start(bf16[256,512]{1,0:T(8,128)(2,1)S(1)} %get-tuple-element.11), channel_id=1, source_target_pairs={{0,16},{2,18},{4,20},{6,22},{8,24},{10,26},{12,28},{14,30},{16,0},... | collective-permute-start | bytes 786440 | tf_op jit(solution)/shard_map/ppermute | solution.py:66
  192.6 29.3 %collective-permute-start = (bf16[256,512]{1,0:T(8,128)(2,1)S(1)}, bf16[256,512]{1,0:T(8,128)(2,1)S(1)}, u32[]{:S(2)}, u32[]{:S(2)}) collective-permute-start(bf16[256,512]{1,0:T(8,128)(2,1)S(1)} %get-tuple-element.9), channel_id=1, source_target_pairs={{0,16},{2,18},{4,20},{6,22},{8,24},{10,26},{12,28},{14,30},{16,0},... | collective-permute-start | bytes 786440 | tf_op jit(solution)/shard_map/ppermute | solution.py:66
  195.5 7.7 %copy-start.3 = (bf16[1,1024,1792]{2,1,0:T(8,128)(2,1)S(1)}, bf16[1,1024,1792]{2,1,0:T(8,128)(2,1)}, u32[]{:S(2)}) copy-start(bf16[1,1024,1792]{2,1,0:T(8,128)(2,1)} %param.12) | copy-start | bytes 11010052
  195.5 33.3 %collective-permute-start.1 = (bf16[256,512]{1,0:T(8,128)(2,1)S(1)}, bf16[256,512]{1,0:T(8,128)(2,1)S(1)}, u32[]{:S(2)}, u32[]{:S(2)}) collective-permute-start(bf16[256,512]{1,0:T(8,128)(2,1)S(1)} %get-tuple-element.10), channel_id=1, source_target_pairs={{0,16},{2,18},{4,20},{6,22},{8,24},{10,26},{12,28},{14,30},{16,0},... | collective-permute-start | bytes 786440 | tf_op jit(solution)/shard_map/ppermute | solution.py:66
Sparse Core Ops, SparseCore 0:
  59.7 4.4 reduce-scatter.11
  104.8 6.6 reduce-scatter.7
  114.3 9.6 reduce-scatter.5
  191.3 75.8 reduce-scatter.9
  269.9 74.2 reduce-scatter.13

commit v2 on v1

--- a/solution.py
+++ b/solution.py
@@ -1,6 +1,8 @@
 import jax
 import jax.numpy as jnp
 from jax import lax
+from jax.experimental import pallas as pl
+from jax.experimental.pallas import tpu as pltpu
 from jax.sharding import PartitionSpec as P
 
 
@@ -21,7 +23,7 @@
     )
 
 
-def per_device(tokens, expert_ids, route_weight, swap_flags, w_gate, w_up, w_down, cotangent):
+def plain_device(tokens, expert_ids, route_weight, swap_flags, w_gate, w_up, w_down, cotangent):
     experts = lax.axis_size("expert")
     half_axis = experts // 2
     my_index = lax.axis_index("expert")
@@ -73,6 +75,343 @@
     return (mixed, input_grad, grads[0][None], grads[1][None], grads[2][None])
 
 
+LANES = 128
+TILE = 256
+ROUTES = 48
+
+
+def layer_kernel(
+    tokens, ids, route, flags, w_gate, w_up, w_down, cotangent,
+    mixed, input_grad, rows, grads, held,
+    gate_w, up_w, down_w, table, weight, total, lean, ours, theirs, outgoing, gate_by, up_by,
+    whole_share, swapped, first_in, second_out, second_in, last_own, last_out, last_in,
+    load_sem, send_sem, recv_sem,
+):
+    depth = rows.shape[0]
+    tok_count, feat = tokens.shape
+    count = depth * 4 * tok_count
+    half = feat // 2
+    share = w_gate.shape[0] // 2
+    me, core = lax.axis_index("expert"), lax.axis_index("dp")
+    z, y, x = me // 4, (me // 2) % 2, me % 2
+    other_x, other_y, other_core = 1 - x, 1 - y, 1 - core
+    low, high = pl.ds(0, half), pl.ds(half, half)
+
+    def place(at_z, at_y, at_x):
+        return {"expert": at_z * 4 + at_y * 2 + at_x}
+
+    beside_x, beside_y, beside_core = place(z, y, other_x), place(z, other_y, x), {"dp": other_core}
+    far = [place(lax.rem(z + step, depth), y, x) for step in range(1, depth)]
+    opposite = place(lax.rem(z + depth // 2, depth), y, x)
+
+    loads = []
+    for number, (source, target) in enumerate(
+        ((w_gate, gate_w), (w_up, up_w), (w_down, down_w))
+    ):
+        loads.append(pltpu.make_async_copy(source, target, load_sem.at[number]))
+        loads[-1].start()
+
+    barrier = pltpu.get_barrier_semaphore()
+    peers = far + [beside_x, beside_y, beside_core]
+    for peer in peers:
+        pl.semaphore_signal(
+            barrier, inc=1, device_id=peer, device_id_type=pl.DeviceIdType.MESH
+        )
+    lanes = lax.broadcasted_iota(jnp.int32, (tok_count, LANES), 1)
+    entry = jnp.zeros((tok_count, LANES), jnp.float32)
+    for choice in range(ids.shape[1]):
+        picked = ids[:, choice : choice + 1] == lanes
+        entry += jnp.where(picked, route[:, choice : choice + 1], 0.0)
+    table[z, y, x] = entry
+    rows[z, y, x] = tokens[...]
+    grads[z, y, x] = cotangent[...]
+    pl.semaphore_wait(barrier, len(peers))
+
+    sent = []
+
+    def push(source, target, device):
+        number = len(sent)
+        copy = pltpu.make_async_remote_copy(
+            src_ref=source,
+            dst_ref=target,
+            send_sem=send_sem.at[number],
+            recv_sem=recv_sem.at[number],
+            device_id=device,
+            device_id_type=pl.DeviceIdType.MESH,
+        )
+        copy.start()
+        sent.append(copy)
+        return copy
+
+    def arrive(copies):
+        for copy in copies:
+            copy.wait_recv()
+
+    def same(ref, device):
+        return push(ref, ref, device)
+
+    def along_z(buffer):
+        return [same(buffer.at[z, y, x], peer) for peer in far]
+
+    def spread_one(buffer):
+        return (
+            same(buffer.at[:, y, x, :, low], beside_x),
+            same(buffer.at[:, y, x, :, high], beside_y),
+        )
+
+    def spread_two(buffer, copies):
+        copies[0].wait_recv()
+        onward = same(buffer.at[:, y, :, :, low], beside_y)
+        copies[1].wait_recv()
+        return onward, same(buffer.at[:, :, x, :, high], beside_x)
+
+    token_z = along_z(rows)
+    table_z = along_z(table)
+    arrive(token_z)
+    grad_z = along_z(grads)
+    token_one = spread_one(rows)
+    arrive(table_z)
+    table_one = same(table.at[:, y, x], beside_x)
+    token_two = spread_two(rows, token_one)
+    table_one.wait_recv()
+    table_two = same(table.at[:, y], beside_y)
+    arrive(grad_z)
+    grad_one = spread_one(grads)
+    arrive(token_two)
+    table_two.wait_recv()
+    every = table[...].reshape(count, LANES)
+    mine = lax.broadcasted_iota(jnp.int32, (count, LANES), 1) == me
+    weight[...] = jnp.broadcast_to(
+        jnp.sum(jnp.where(mine, every, 0.0), axis=1, keepdims=True), (count, LANES)
+    )
+
+    def project(buffer, matrix, first, target):
+        def tile(step, carry):
+            units = pl.ds(pl.multiple_of(first + step * TILE, TILE), TILE)
+            columns = pl.ds(pl.multiple_of(step * TILE, TILE), TILE)
+            target[:, columns] = contract_last(
+                buffer[...].reshape(count, feat), matrix[units, :]
+            )
+            return carry
+
+        lax.fori_loop(0, share // TILE, tile, 0)
+
+    def partial(number, buffer, matrix):
+        project(buffer, matrix, other_core * share, outgoing.at[number])
+        return push(outgoing.at[number], theirs.at[number], beside_core)
+
+    loads[0].wait()
+    gate_sum = partial(0, rows, gate_w)
+    loads[1].wait()
+    up_sum = partial(1, rows, up_w)
+    project(rows, gate_w, core * share, ours.at[0])
+    grad_two = spread_two(grads, grad_one)
+    project(rows, up_w, core * share, ours.at[1])
+    loads[2].wait()
+    arrive((gate_sum, up_sum))
+
+    chunk = 2 * tok_count
+
+    def activate(step, carry):
+        part = pl.ds(pl.multiple_of(step * chunk, chunk), chunk)
+        scale = weight[part, 0:1]
+        up_value = ours[1, part, :] + theirs[1, part, :]
+        activated, slope = silu_parts(ours[0, part, :] + theirs[0, part, :])
+        hidden = activated * up_value
+        whole_share[0, core, part, :] = hidden.astype(jnp.bfloat16)
+        swapped[0, part, :] = (scale * hidden).astype(jnp.bfloat16)
+        gate_by[part, :] = scale * up_value * slope
+        up_by[part, :] = scale * activated
+        return carry
+
+    lax.fori_loop(0, count // chunk, activate, 0)
+    hidden_share = same(whole_share.at[0, core], beside_core)
+    trades = [push(swapped.at[0], swapped.at[1], opposite)]
+    hidden_share.wait_recv()
+
+    def combine(number, terms, scaled):
+        def tile(step, carry):
+            columns = pl.ds(pl.multiple_of(step * TILE, TILE), TILE)
+            result = jnp.zeros((count, TILE), jnp.float32)
+            for source, matrix in terms:
+                for side in range(2):
+                    result += jnp.dot(
+                        whole_share[source, side],
+                        matrix[side * share : (side + 1) * share, columns],
+                        preferred_element_type=jnp.float32,
+                    )
+            if scaled:
+                result = result * weight[:, 0:1]
+            result = result.reshape(depth, 2, 2, tok_count, TILE)
+            total[number, :, :, :, :, columns] = result
+            lean[number, :, :, :, :, columns] = result.astype(jnp.bfloat16)
+            return carry
+
+        lax.fori_loop(0, feat // TILE, tile, 0)
+
+    def reduce_one(number):
+        return (
+            push(lean.at[number, :, other_y, :, :, low], first_in.at[number, 0], beside_y),
+            push(lean.at[number, :, :, other_x, :, high], first_in.at[number, 1], beside_x),
+        )
+
+    def reduce_two(number, copies):
+        copies[0].wait_recv()
+        second_out[number, 0] = (
+            total[number, :, y, other_x, :, low]
+            + first_in[number, 0, :, other_x].astype(jnp.float32)
+        ).astype(jnp.bfloat16)
+        onward = push(second_out.at[number, 0], second_in.at[number, 0], beside_x)
+        copies[1].wait_recv()
+        second_out[number, 1] = (
+            total[number, :, other_y, x, :, high]
+            + first_in[number, 1, :, other_y].astype(jnp.float32)
+        ).astype(jnp.bfloat16)
+        return onward, push(second_out.at[number, 1], second_in.at[number, 1], beside_y)
+
+    def reduce_three(number, copies):
+        arrive(copies)
+        for side, (columns, index) in enumerate(((low, x), (high, y))):
+            result = (
+                total[number, :, y, x, :, columns]
+                + first_in[number, side, :, index].astype(jnp.float32)
+                + second_in[number, side].astype(jnp.float32)
+            )
+            last_own[number, :, :, columns] = result
+            last_out[number, :, :, columns] = result.astype(jnp.bfloat16)
+        return [
+            push(
+                last_out.at[number, lax.rem(z + step, depth)],
+                last_in.at[number, step - 1],
+                far[step - 1],
+            )
+            for step in range(1, depth)
+        ]
+
+    def reduce_end(number, copies, target):
+        arrive(copies)
+        result = last_own[number, z]
+        for step in range(depth - 1):
+            result += last_in[number, step].astype(jnp.float32)
+        target[...] = result.astype(jnp.bfloat16)
+
+    combine(0, ((0, down_w),), True)
+    mixed_one = reduce_one(0)
+    arrive(grad_two)
+    grad_sum = partial(2, grads, down_w)
+    project(grads, down_w, core * share, ours.at[2])
+    grad_sum.wait_recv()
+
+    def backward(step, carry):
+        part = pl.ds(pl.multiple_of(step * chunk, chunk), chunk)
+        hidden_grad = ours[2, part, :] + theirs[2, part, :]
+        whole_share[1, core, part, :] = (hidden_grad * gate_by[part, :]).astype(jnp.bfloat16)
+        whole_share[2, core, part, :] = (hidden_grad * up_by[part, :]).astype(jnp.bfloat16)
+        return carry
+
+    lax.fori_loop(0, count // chunk, backward, 0)
+    gate_share = same(whole_share.at[1, core], beside_core)
+    up_share = same(whole_share.at[2, core], beside_core)
+    trades.append(push(whole_share.at[1, core], swapped.at[2], opposite))
+    trades.append(push(whole_share.at[2, core], swapped.at[3], opposite))
+    mixed_two = reduce_two(0, mixed_one)
+    arrive((gate_share, up_share))
+    combine(1, ((1, gate_w), (2, up_w)), False)
+    back_one = reduce_one(1)
+    mixed_three = reduce_three(0, mixed_two)
+    back_two = reduce_two(1, back_one)
+    back_three = reduce_three(1, back_two)
+
+    flag = flags[0, me % (2 * depth)] == 1
+    kept = []
+    for number in range(3):
+        trades[number].wait_recv()
+        own = swapped[0] if number == 0 else whole_share[number, core]
+        held[number, core] = jnp.where(flag, swapped[number + 1], own)
+        kept.append(same(held.at[number, core], beside_core))
+    reduce_end(0, mixed_three, mixed)
+    reduce_end(1, back_three, input_grad)
+    arrive(kept)
+    for copy in sent:
+        copy.wait_send()
+
+
+def kernel_device(tokens, expert_ids, route_weight, swap_flags, w_gate, w_up, w_down, cotangent):
+    tok_count, feat = tokens.shape
+    depth = lax.axis_size("expert") // 4
+    count = depth * 4 * tok_count
+    units = w_gate.shape[1]
+    share = units // 2
+    half = feat // 2
+    narrow, wide = jnp.bfloat16, jnp.float32
+    grid = (depth, 2, 2, tok_count)
+    vmem = pl.BlockSpec(memory_space=pltpu.VMEM)
+    smem = pl.BlockSpec(memory_space=pltpu.SMEM)
+    hbm = pl.BlockSpec(memory_space=pl.ANY)
+    mixed, input_grad, rows, grads, held = pl.pallas_call(
+        layer_kernel,
+        out_shape=(
+            jax.ShapeDtypeStruct((tok_count, feat), narrow),
+            jax.ShapeDtypeStruct((tok_count, feat), narrow),
+            jax.ShapeDtypeStruct(grid + (feat,), narrow),
+            jax.ShapeDtypeStruct(grid + (feat,), narrow),
+            jax.ShapeDtypeStruct((3, 2, count, share), narrow),
+        ),
+        in_specs=[vmem, vmem, vmem, smem, hbm, hbm, hbm, vmem],
+        out_specs=(vmem,) * 5,
+        scratch_shapes=[
+            pltpu.VMEM((units, feat), narrow),
+            pltpu.VMEM((units, feat), narrow),
+            pltpu.VMEM((units, feat), narrow),
+            pltpu.VMEM(grid + (LANES,), wide),
+            pltpu.VMEM((count, LANES), wide),
+            pltpu.VMEM((2,) + grid + (feat,), wide),
+            pltpu.VMEM((2,) + grid + (feat,), narrow),
+            pltpu.VMEM((3, count, share), wide),
+            pltpu.VMEM((3, count, share), wide),
+            pltpu.VMEM((3, count, share), wide),
+            pltpu.VMEM((count, share), wide),
+            pltpu.VMEM((count, share), wide),
+            pltpu.VMEM((3, 2, count, share), narrow),
+            pltpu.VMEM((4, count, share), narrow),
+            pltpu.VMEM((2, 2, depth, 2, tok_count, half), narrow),
+            pltpu.VMEM((2, 2, depth, tok_count, half), narrow),
+            pltpu.VMEM((2, 2, depth, tok_count, half), narrow),
+            pltpu.VMEM((2, depth, tok_count, feat), wide),
+            pltpu.VMEM((2, depth, tok_count, feat), narrow),
+            pltpu.VMEM((2, depth - 1, tok_count, feat), narrow),
+            pltpu.SemaphoreType.DMA((3,)),
+            pltpu.SemaphoreType.DMA((ROUTES,)),
+            pltpu.SemaphoreType.DMA((ROUTES,)),
+        ],
+        compiler_params=pltpu.CompilerParams(
+            collective_id=0, has_side_effects=True, vmem_limit_bytes=56 * 2**20
+        ),
+    )(
+        tokens, expert_ids, route_weight, swap_flags[None], w_gate[0], w_up[0], w_down[0],
+        cotangent,
+    )
+    rows, grads = rows.reshape(count, feat), grads.reshape(count, feat)
+
+    def outer(operand, other):
+        product = lax.dot_general(
+            operand, other, (((1,), (0,)), ((), ())), preferred_element_type=jnp.float32
+        )
+        return product.astype(narrow).reshape(1, units, feat)
+
+    return mixed, input_grad, outer(held[1], rows), outer(held[2], rows), outer(held[0], grads)
+
+
+def per_device(*operands):
+    experts, shards = lax.axis_size("expert"), lax.axis_size("dp")
+    tok_count, feat = operands[0].shape
+    units = operands[4].shape[1]
+    fits = 8 <= experts <= 16 and experts % 8 == 0 and shards == 2 and tok_count % 16 == 0
+    fits = fits and feat % TILE == 0 and units % (2 * TILE) == 0
+    fits = fits and 3 * units * feat <= 6 * 2**20 and experts * tok_count <= 256
+    return kernel_device(*operands) if fits else plain_device(*operands)
+
+
 def solution(mesh):
     return jax.shard_map(
         per_device,

time: 351 us -> 91 us (0.26)
  blocking collectives: 176 us -> 0 us
  waiting for transfers between devices: 123 us -> 0 us
  Pallas kernels: 0 us -> 75.6 us
  matrix products: 30.9 us -> 10.5 us
  between operations: 14.6 us -> 0.66 us
    all_gather x10 -> x0, blocking collectives: 176 us -> none  [the longest x1 48.1 us: per_device(): grad_rows = lax.all_gather(cotangent, 'expert', axis=0, tiled=True)]
    reduce_scatter x5 -> x0, waiting for transfers between devices: 104 us -> none  [the longest x1 76.9 us: per_device(): lax.psum_scatter(back_part.astype(jnp.bfloat16), 'expert', scatter_dimens...]
    pallas_call x0 -> x1, Pallas kernels: none -> 75.6 us  [kernel_device(): pl.pallas_call(layer_kernel, out_shape=(jax.ShapeDtypeStruct((tok_count,...]
    dot_general x9 -> x3, matrix products: 30.9 us -> 10.5 us  [outer(): lax.dot_general(operand, other, (((1,), (0,)), ((), ())), preferred_eleme...]
    ppermute x3 -> x0, waiting for transfers between devices: 19 us -> none  [held(): lax.ppermute(share, 'expert', pairs)]
    unnamed x10 -> x14, local copies, waits for them, and re-layouts: 0.02 us -> 3.97 us
  transfers between devices with their start and end apart: 8 -> 0, of which waited for: 5 -> 0; matrix products, arithmetic and copies ran while one was open for 7% -> 0% of each run, Pallas kernels for 0% -> 0%
where the time goes in v2:
time: 91 us; the launch traced here: 90.8 us
  Pallas kernels  75.6 us (83%)
  matrix products  10.5 us (12%)
  local copies, waits for them, and re-layouts  3.97 us (4%)
    pallas_call x1, Pallas kernels, kernel_device(): pl.pallas_call(layer_kernel, out_shape=(jax.ShapeDtypeStruct((tok_count,...  75.6 us
    dot_general x3, matrix products, outer(): lax.dot_general(operand, other, (((1,), (0,)), ((), ())), preferred_eleme...  10.5 us
    unnamed x14, local copies, waits for them, and re-layouts  3.97 us

profile of v2, /device:TPU:0, one launch (start us, length us, event | category | flops | bytes accessed | tf_op | source)
XLA Modules:
  0.0 90.8 jit_solution(5875711116648111852)
XLA Ops:
  0.6 1.4 %copy.13.ids = s32[16,8]{1,0:T(8,128)} copy(s32[16,8]{0,1:T(8,128)} %param.9) | data formatting | bytes 1024 | tf_op args[1]
  2.0 1.4 %copy.14.route = f32[16,8]{1,0:T(8,128)} copy(f32[16,8]{0,1:T(8,128)} %param.10) | data formatting | bytes 1024 | tf_op args[2]
  3.3 75.6 %shard_map.119 = (bf16[16,1792]{1,0:T(8,128)(2,1)}, bf16[16,1792]{1,0:T(8,128)(2,1)}, bf16[4,2,2,16,1792]{4,3,2,1,0:T(8,128)(2,1)}, bf16[4,2,2,16,1792]{4,3,2,1,0:T(8,128)(2,1)}, bf16[3,2,256,512]{3,2,1,0:T(8,128)(2,1)}) custom-call(bf16[16,1792]{1,0:T(8,128)(2,1)} %tokens.1, s32[16,8]{1,0:T(8,128)} %copy.13.ids, f32[16,8]{1,0:T(8,128)} %copy.14.route, ...), custom_call_target="tpu_custom_call" | custom-call | tf_op jit(solution)/shard_map/pallas_call | solution.py:351
  79.0 0.0 copy-start
  79.0 0.0 copy-start.2
  79.0 4.5 %convolution_convert_fusion.1 = bf16[2,512,1792]{2,1,0:T(8,128)(2,1)} fusion(bf16[256,1792,1]{1,0,2:T(8,128)(2,1)} %bitcast.31, bf16[3,2,256,512]{3,2,1,0:T(8,128)(2,1)} %get-tuple-element.12), kind=kOutput, calls=%fused_computation.1 | convolution fusion | flops 941359104 | bytes 5111808 | tf_op jit(solution)/shard_map/dot_general | solution.py:397
  83.5 0.0 copy-start.1
  83.5 0.0 copy-done
  83.5 0.0 copy-done.2
  83.5 3.0 %convolution_convert_fusion = bf16[2,512,1792]{2,1,0:T(8,128)(2,1)} fusion(bf16[256,1792,1]{1,0,2:T(8,128)(2,1)S(1)} %bitcast.33, bf16[3,2,256,512]{3,2,1,0:T(8,128)(2,1)S(1)} %copy-done), kind=kOutput, calls=%fused_computation | convolution fusion | flops 941359104 | bytes 5111808 | tf_op jit(solution)/shard_map/dot_general | solution.py:397
  86.5 0.0 copy-start.4
  86.5 0.0 copy-start.3
  86.5 0.0 copy-done.1
  86.5 3.0 %convolution_convert_fusion.2 = bf16[2,512,1792]{2,1,0:T(8,128)(2,1)} fusion(bf16[256,1792,1]{1,0,2:T(8,128)(2,1)S(1)} %bitcast.32, bf16[3,2,256,512]{3,2,1,0:T(8,128)(2,1)S(1)} %copy-done), kind=kOutput, calls=%fused_computation.2 | convolution fusion | flops 941359104 | bytes 5111808 | tf_op jit(solution)/shard_map/dot_general | solution.py:397
  89.5 0.0 copy-done.4
  89.5 0.6 copy.23
  90.1 0.0 copy-done.3
  90.2 0.6 copy.24
Async XLA Ops:
  79.0 4.5 %copy-start = (bf16[3,2,256,512]{3,2,1,0:T(8,128)(2,1)S(1)}, bf16[3,2,256,512]{3,2,1,0:T(8,128)(2,1)}, u32[]{:S(2)}) copy-start(bf16[3,2,256,512]{3,2,1,0:T(8,128)(2,1)} %get-tuple-element.12) | copy-start | bytes 4718596
  79.0 4.5 %copy-start.2 = (bf16[4,2,2,16,1792]{4,3,2,1,0:T(8,128)(2,1)S(1)}, bf16[4,2,2,16,1792]{4,3,2,1,0:T(8,128)(2,1)}, u32[]{:S(2)}) copy-start(bf16[4,2,2,16,1792]{4,3,2,1,0:T(8,128)(2,1)} %get-tuple-element.14) | copy-start | bytes 2752516
  83.5 3.0 %copy-start.1 = (bf16[4,2,2,16,1792]{4,3,2,1,0:T(8,128)(2,1)S(1)}, bf16[4,2,2,16,1792]{4,3,2,1,0:T(8,128)(2,1)}, u32[]{:S(2)}) copy-start(bf16[4,2,2,16,1792]{4,3,2,1,0:T(8,128)(2,1)} %get-tuple-element.13) | copy-start | bytes 2752516
  86.5 3.0 %copy-start.4 = (bf16[16,1792]{1,0:T(8,128)(2,1)S(1)}, bf16[16,1792]{1,0:T(8,128)(2,1)}, u32[]{:S(2)}) copy-start(bf16[16,1792]{1,0:T(8,128)(2,1)} %get-tuple-element.20) | copy-start | bytes 172036
  86.5 3.6 %copy-start.3 = (bf16[16,1792]{1,0:T(8,128)(2,1)S(1)}, bf16[16,1792]{1,0:T(8,128)(2,1)}, u32[]{:S(2)}) copy-start(bf16[16,1792]{1,0:T(8,128)(2,1)} %get-tuple-element.21) | copy-start | bytes 172036

commit v3 on v2

--- a/solution.py
+++ b/solution.py
@@ -117,12 +117,17 @@
         pl.semaphore_signal(
             barrier, inc=1, device_id=peer, device_id_type=pl.DeviceIdType.MESH
         )
-    lanes = lax.broadcasted_iota(jnp.int32, (tok_count, LANES), 1)
-    entry = jnp.zeros((tok_count, LANES), jnp.float32)
-    for choice in range(ids.shape[1]):
-        picked = ids[:, choice : choice + 1] == lanes
-        entry += jnp.where(picked, route[:, choice : choice + 1], 0.0)
-    table[z, y, x] = entry
+    experts = lax.broadcasted_iota(jnp.int32, (LANES, tok_count), 0)
+    entry = jnp.zeros((LANES, tok_count), jnp.float32)
+    for choice in range(ids.shape[0]):
+        picked = ids[choice : choice + 1, :] == experts
+        entry += jnp.where(picked, route[choice : choice + 1, :], 0.0)
+    token = lax.broadcasted_iota(jnp.int32, (tok_count, tok_count), 0)
+    unit = token == lax.broadcasted_iota(jnp.int32, (tok_count, tok_count), 1)
+    table[z, y, x] = lax.dot_general(
+        unit.astype(jnp.float32), entry, (((1,), (1,)), ((), ())),
+        precision=lax.Precision.HIGHEST, preferred_element_type=jnp.float32,
+    )
     rows[z, y, x] = tokens[...]
     grads[z, y, x] = cotangent[...]
     pl.semaphore_wait(barrier, len(peers))
@@ -227,7 +232,6 @@
     lax.fori_loop(0, count // chunk, activate, 0)
     hidden_share = same(whole_share.at[0, core], beside_core)
     trades = [push(swapped.at[0], swapped.at[1], opposite)]
-    hidden_share.wait_recv()
 
     def combine(number, terms, scaled):
         def tile(step, carry):
@@ -295,8 +299,6 @@
             result += last_in[number, step].astype(jnp.float32)
         target[...] = result.astype(jnp.bfloat16)
 
-    combine(0, ((0, down_w),), True)
-    mixed_one = reduce_one(0)
     arrive(grad_two)
     grad_sum = partial(2, grads, down_w)
     project(grads, down_w, core * share, ours.at[2])
@@ -314,10 +316,13 @@
     up_share = same(whole_share.at[2, core], beside_core)
     trades.append(push(whole_share.at[1, core], swapped.at[2], opposite))
     trades.append(push(whole_share.at[2, core], swapped.at[3], opposite))
-    mixed_two = reduce_two(0, mixed_one)
+    hidden_share.wait_recv()
+    combine(0, ((0, down_w),), True)
+    mixed_one = reduce_one(0)
     arrive((gate_share, up_share))
     combine(1, ((1, gate_w), (2, up_w)), False)
     back_one = reduce_one(1)
+    mixed_two = reduce_two(0, mixed_one)
     mixed_three = reduce_three(0, mixed_two)
     back_two = reduce_two(1, back_one)
     back_three = reduce_three(1, back_two)
@@ -388,18 +393,39 @@
             collective_id=0, has_side_effects=True, vmem_limit_bytes=56 * 2**20
         ),
     )(
-        tokens, expert_ids, route_weight, swap_flags[None], w_gate[0], w_up[0], w_down[0],
+        tokens, expert_ids.T, route_weight.T, swap_flags[None], w_gate[0], w_up[0], w_down[0],
         cotangent,
     )
     rows, grads = rows.reshape(count, feat), grads.reshape(count, feat)
-
-    def outer(operand, other):
-        product = lax.dot_general(
-            operand, other, (((1,), (0,)), ((), ())), preferred_element_type=jnp.float32
-        )
-        return product.astype(narrow).reshape(1, units, feat)
-
-    return mixed, input_grad, outer(held[1], rows), outer(held[2], rows), outer(held[0], grads)
+    tile = min(TILE, share)
+    tiles = share // tile
+    whole_rows = pl.BlockSpec((count, feat), lambda step: (0, 0))
+    block = pl.BlockSpec((1, tile, feat), lambda step: (0, step, 0))
+    gate, up, down = pl.pallas_call(
+        outer_kernel,
+        grid=(2 * tiles,),
+        out_shape=(jax.ShapeDtypeStruct((1, units, feat), narrow),) * 3,
+        in_specs=[
+            pl.BlockSpec(
+                (3, 1, count, tile), lambda step: (0, step // tiles, 0, lax.rem(step, tiles))
+            ),
+            whole_rows,
+            whole_rows,
+        ],
+        out_specs=(block,) * 3,
+        compiler_params=pltpu.CompilerParams(vmem_limit_bytes=56 * 2**20),
+        cost_estimate=pl.CostEstimate(
+            flops=6 * count * units * feat,
+            bytes_accessed=6 * units * (feat + count) + 4 * count * feat,
+            transcendentals=0,
+        ),
+    )(held, rows, grads)
+    return mixed, input_grad, gate, up, down
+
+
+def outer_kernel(held, rows, grads, gate, up, down):
+    for number, other, target in ((1, rows, gate), (2, rows, up), (0, grads, down)):
+        target[0] = contract_first(held[number, 0], other[...]).astype(jnp.bfloat16)
 
 
 def per_device(*operands):

time: 91 us -> 84.7 us (0.931)
  matrix products: 10.5 us -> 0 us
  Pallas kernels: 75.6 us -> 82.5 us
  local copies, waits for them, and re-layouts: 3.97 us -> 1.25 us
    dot_general x3 -> x0, matrix products: 10.5 us -> none  [outer(): lax.dot_general(operand, other, (((1,), (0,)), ((), ())), preferred_eleme...]
    pallas_call x0 -> x1, Pallas kernels: none -> 6.88 us  [kernel_device(): pl.pallas_call(outer_kernel, grid=(2 * tiles,), out_shape=(jax.ShapeDtype...]
    unnamed x14 -> x6, local copies, waits for them, and re-layouts: 3.97 us -> 1.25 us
where the time goes in v3:
time: 84.7 us; the launch traced here: 84.4 us
  Pallas kernels  82.5 us (97%)
  local copies, waits for them, and re-layouts  1.25 us (1%)
    pallas_call x1, Pallas kernels, kernel_device(): pl.pallas_call(layer_kernel, out_shape=(jax.ShapeDtypeStruct((tok_count,...  75.6 us
    pallas_call x1, Pallas kernels, kernel_device(): pl.pallas_call(outer_kernel, grid=(2 * tiles,), out_shape=(jax.ShapeDtype...  6.88 us

profile of v3, /device:TPU:0, one launch (start us, length us, event | category | flops | bytes accessed | tf_op | source)
XLA Modules:
  0.0 84.4 jit_solution(2524633437874558893)
XLA Ops:
  0.6 75.6 %shard_map.119 = (bf16[16,1792]{1,0:T(8,128)(2,1)}, bf16[16,1792]{1,0:T(8,128)(2,1)}, bf16[4,2,2,16,1792]{4,3,2,1,0:T(8,128)(2,1)}, bf16[4,2,2,16,1792]{4,3,2,1,0:T(8,128)(2,1)}, bf16[3,2,256,512]{3,2,1,0:T(8,128)(2,1)}) custom-call(bf16[16,1792]{1,0:T(8,128)(2,1)} %tokens.1, s32[8,16]{1,0:T(8,128)} %bitcast.11, f32[8,16]{1,0:T(8,128)} %bitcast.12, ...), custom_call_target="tpu_custom_call" | custom-call | tf_op jit(solution)/shard_map/pallas_call | solution.py:356
  76.3 0.0 copy-start.1
  76.3 0.0 copy-start
  76.3 6.9 %shard_map.120 = (bf16[1,1024,1792]{2,1,0:T(8,128)(2,1)}, bf16[1,1024,1792]{2,1,0:T(8,128)(2,1)}, bf16[1,1024,1792]{2,1,0:T(8,128)(2,1)}) custom-call(bf16[3,2,256,512]{3,2,1,0:T(8,128)(2,1)} %get-tuple-element.15.held, bf16[256,1792]{1,0:T(8,128)(2,1)} %bitcast.14, bf16[256,1792]{1,0:T(8,128)(2,1)} %bitcast.15), custom_call_target="tpu_custom_call" | custom-call | flops 2818572288 | bytes 14417920 | tf_op jit(solution)/shard_map/pallas_call | solution.py:404
  83.2 0.0 copy-done.1
  83.2 0.6 copy.15
  83.8 0.0 copy-done
  83.8 0.6 copy.16
Async XLA Ops:
  76.3 6.9 %copy-start.1 = (bf16[16,1792]{1,0:T(8,128)(2,1)S(1)}, bf16[16,1792]{1,0:T(8,128)(2,1)}, u32[]{:S(2)}) copy-start(bf16[16,1792]{1,0:T(8,128)(2,1)} %get-tuple-element.26) | copy-start | bytes 172036
  76.3 7.5 %copy-start = (bf16[16,1792]{1,0:T(8,128)(2,1)S(1)}, bf16[16,1792]{1,0:T(8,128)(2,1)}, u32[]{:S(2)}) copy-start(bf16[16,1792]{1,0:T(8,128)(2,1)} %get-tuple-element.27) | copy-start | bytes 172036

commit v4 on v3

--- a/solution.py
+++ b/solution.py
@@ -77,7 +77,7 @@
 
 LANES = 128
 TILE = 256
-ROUTES = 48
+ROUTES = 96
 
 
 def layer_kernel(
@@ -158,30 +158,36 @@
     def along_z(buffer):
         return [same(buffer.at[z, y, x], peer) for peer in far]
 
-    def spread_one(buffer):
-        return (
-            same(buffer.at[:, y, x, :, low], beside_x),
-            same(buffer.at[:, y, x, :, high], beside_y),
-        )
+    def spread_one(buffer, arriving):
+        copies = []
+        for step in range(depth):
+            if step:
+                arriving[step - 1].wait_recv()
+            at_z = lax.rem(z - step + depth, depth)
+            by_x = same(buffer.at[at_z, y, x, :, low], beside_x)
+            by_y = same(buffer.at[at_z, y, x, :, high], beside_y)
+            copies.append((at_z, by_x, by_y))
+        return copies
 
     def spread_two(buffer, copies):
-        copies[0].wait_recv()
-        onward = same(buffer.at[:, y, :, :, low], beside_y)
-        copies[1].wait_recv()
-        return onward, same(buffer.at[:, :, x, :, high], beside_x)
+        onward = []
+        for at_z, by_x, by_y in copies:
+            by_x.wait_recv()
+            onward.append(same(buffer.at[at_z, y, :, :, low], beside_y))
+            by_y.wait_recv()
+            onward.append(same(buffer.at[at_z, :, x, :, high], beside_x))
+        return onward
 
     token_z = along_z(rows)
     table_z = along_z(table)
-    arrive(token_z)
+    token_one = spread_one(rows, token_z)
     grad_z = along_z(grads)
-    token_one = spread_one(rows)
     arrive(table_z)
     table_one = same(table.at[:, y, x], beside_x)
     token_two = spread_two(rows, token_one)
     table_one.wait_recv()
     table_two = same(table.at[:, y], beside_y)
-    arrive(grad_z)
-    grad_one = spread_one(grads)
+    grad_one = spread_one(grads, grad_z)
     arrive(token_two)
     table_two.wait_recv()
     every = table[...].reshape(count, LANES)

time: 84.7 us -> 83.9 us (level)
  no operation moved by 1% of the time
where the time goes in v4:
time: 83.9 us; the launch traced here: 83.6 us
  Pallas kernels  81.7 us (97%)
  local copies, waits for them, and re-layouts  1.25 us (1%)
    pallas_call x1, Pallas kernels, kernel_device(): pl.pallas_call(layer_kernel, out_shape=(jax.ShapeDtypeStruct((tok_count,...  74.8 us
    pallas_call x1, Pallas kernels, kernel_device(): pl.pallas_call(outer_kernel, grid=(2 * tiles,), out_shape=(jax.ShapeDtype...  6.88 us

profile of v4, /device:TPU:0, one launch (start us, length us, event | category | flops | bytes accessed | tf_op | source)
XLA Modules:
  0.0 83.6 jit_solution(9382117052162579358)
XLA Ops:
  0.6 74.8 %shard_map.119 = (bf16[16,1792]{1,0:T(8,128)(2,1)}, bf16[16,1792]{1,0:T(8,128)(2,1)}, bf16[4,2,2,16,1792]{4,3,2,1,0:T(8,128)(2,1)}, bf16[4,2,2,16,1792]{4,3,2,1,0:T(8,128)(2,1)}, bf16[3,2,256,512]{3,2,1,0:T(8,128)(2,1)}) custom-call(bf16[16,1792]{1,0:T(8,128)(2,1)} %tokens.1, s32[8,16]{1,0:T(8,128)} %bitcast.11, f32[8,16]{1,0:T(8,128)} %bitcast.12, ...), custom_call_target="tpu_custom_call" | custom-call | tf_op jit(solution)/shard_map/pallas_call | solution.py:362
  75.4 0.0 copy-start.1
  75.4 0.0 copy-start
  75.5 6.9 %shard_map.120 = (bf16[1,1024,1792]{2,1,0:T(8,128)(2,1)}, bf16[1,1024,1792]{2,1,0:T(8,128)(2,1)}, bf16[1,1024,1792]{2,1,0:T(8,128)(2,1)}) custom-call(bf16[3,2,256,512]{3,2,1,0:T(8,128)(2,1)} %get-tuple-element.15.held, bf16[256,1792]{1,0:T(8,128)(2,1)} %bitcast.14, bf16[256,1792]{1,0:T(8,128)(2,1)} %bitcast.15), custom_call_target="tpu_custom_call" | custom-call | flops 2818572288 | bytes 14417920 | tf_op jit(solution)/shard_map/pallas_call | solution.py:410
  82.3 0.0 copy-done.1
  82.3 0.6 copy.15
  83.0 0.0 copy-done
  83.0 0.6 copy.16
Async XLA Ops:
  75.4 6.9 %copy-start.1 = (bf16[16,1792]{1,0:T(8,128)(2,1)S(1)}, bf16[16,1792]{1,0:T(8,128)(2,1)}, u32[]{:S(2)}) copy-start(bf16[16,1792]{1,0:T(8,128)(2,1)} %get-tuple-element.26) | copy-start | bytes 172036
  75.4 7.5 %copy-start = (bf16[16,1792]{1,0:T(8,128)(2,1)S(1)}, bf16[16,1792]{1,0:T(8,128)(2,1)}, u32[]{:S(2)}) copy-start(bf16[16,1792]{1,0:T(8,128)(2,1)} %get-tuple-element.27) | copy-start | bytes 172036
